TPU v7x, 32 devices: a whole 2x2x4 slice. The times are simulated.
32 devices in a mesh: gx: 8 (over z, x), gz: 4 (over y, core).
Axes of the slice: x: 2, y: 2, z: 4, core: 2. Of those that a mesh axis runs over, the one named last changes fastest.
Arguments:
- rhs_field: float32 [256, 32, 1024], P('gz', None, 'gx'), may hold values from -6 to 6
- heights: int32 [1024, 32], P('gx'), may hold values from 0 to 63
- vert_coef: float32 [256], replicated, may hold values from 30 to 300
- balance: int32 [8, 32], P('gx'), may hold values from 0 to 31, each once within a row
Outputs:
- pressure: float32 [256, 32, 1024], P('gz', None, 'gx')
- coarse_bundles: float32 [256, 4096], P('gx', 'gz')
Inputs may be any that keep to these rules, and one draw needn't show every extreme that they name: `heights`: cells of a column below its height are inside a building. `balance`: each row lists every one of the 32 bundles of one source once.
All inputs are finite; a program needn't handle non-finite values.
Results may differ from a plain program's by a relative error of at most 0.0008.
Values sent between devices are 32-bit elements; how exact they have to be, the bound alone decides.
A program may use at most 128 MiB of HBM per device.

v0:
```python
import jax
import jax.numpy as jnp
from jax import lax
from jax.sharding import PartitionSpec as P

SWEEPS = 2


def extended(cells, sides, width):
    for axis, dim in sides:
        count = lax.axis_size(axis)
        ends = count - 1
        head = lax.slice_in_dim(cells, 0, width, axis=dim)
        tail = lax.slice_in_dim(cells, cells.shape[dim] - width, cells.shape[dim], axis=dim)
        cells = jnp.concatenate(
            [
                lax.ppermute(tail, axis, [(i, (i + 1) % count) for i in range(ends)]),
                cells,
                lax.ppermute(head, axis, [((i + 1) % count, i) for i in range(ends)]),
            ],
            axis=dim,
        )
    return cells


def shifted(values, stride, fill_value):
    length = values.shape[0]
    padding = jnp.full((abs(stride),) + values.shape[1:], fill_value, values.dtype)
    if stride > 0:
        return jnp.concatenate([padding, values[: length - stride]], 0)
    return jnp.concatenate([values[-stride:], padding], 0)


def cyclic_solve(lower_band, centre, upper_band, right_sides):
    length = centre.shape[0]
    stride = 1
    while stride < length:
        factor_low = -lower_band / shifted(centre, stride, 1.0)
        factor_high = -upper_band / shifted(centre, -stride, 1.0)
        right_sides = tuple(
            (
                side
                + factor_low * shifted(side, stride, 0.0)
                + factor_high * shifted(side, -stride, 0.0)
                for side in right_sides
            )
        )
        new_centre = (
            centre
            + factor_low * shifted(upper_band, stride, 0.0)
            + factor_high * shifted(lower_band, -stride, 0.0)
        )
        lower_band = factor_low * shifted(lower_band, stride, 0.0)
        upper_band = factor_high * shifted(upper_band, -stride, 0.0)
        centre = new_centre
        stride = stride * 2
    return tuple((side / centre for side in right_sides))


def line_bands(below_coef, above_coef, fluid_mask):
    below_full = below_coef[:, None, None] * fluid_mask
    above_full = above_coef[:, None, None] * fluid_mask
    centre = fluid_mask * (4.0 + below_coef[:, None, None] + above_coef[:, None, None]) + (
        1.0 - fluid_mask
    )
    return (-below_full, centre, -above_full)


def horizontal_sum(padded):
    return padded[:, 1:-1, :-2] + padded[:, 1:-1, 2:] + padded[:, :-2, 1:-1] + padded[:, 2:, 1:-1]


def pick_colour(values, parity):
    paired = values.reshape(values.shape[:-1] + (values.shape[-1] // 2, 2))
    return jnp.where(parity[:, None] == 0, paired[..., 0], paired[..., 1])


def put_colour(values, chosen, parity):
    paired = values.reshape(values.shape[:-1] + (values.shape[-1] // 2, 2))
    slot_ids = jnp.arange(2, dtype=jnp.int32)
    placed = jnp.where(parity[:, None, None] == slot_ids, chosen[..., None], paired)
    return placed.reshape(values.shape)


def column_sweep(pressure, rhs_cols, fluid_cols, bands, parity):
    padded = extended(pressure, (("gx", 2), ("gz", 1)), 1)
    right_side = fluid_cols * (rhs_cols + horizontal_sum(padded))
    lower_band, centre, upper_band = (pick_colour(band, parity) for band in bands)
    (solved,) = cyclic_solve(lower_band, centre, upper_band, (pick_colour(right_side, parity),))
    return put_colour(pressure, solved, parity)


def on_device(rhs_field, heights, vert_coef, balance):
    slab_z, rows_y, width_x = rhs_field.shape
    layer_pos = lax.axis_index("gz")
    first_level = layer_pos * slab_z
    padded_coef = jnp.concatenate([vert_coef, jnp.zeros((1,), jnp.float32)])
    below_slab = lax.dynamic_slice_in_dim(padded_coef, first_level, slab_z)
    above_slab = lax.dynamic_slice_in_dim(padded_coef, first_level + 1, slab_z)
    level_ids = first_level + jnp.arange(slab_z, dtype=jnp.int32)
    fluid_slab = (level_ids[:, None, None] >= heights.T[None]).astype(jnp.float32)
    rhs_cols = lax.all_to_all(rhs_field, "gz", split_axis=1, concat_axis=0, tiled=True)
    total_z, band_y, width_cols = rhs_cols.shape
    row_first = layer_pos * band_y
    band_heights = lax.dynamic_slice_in_dim(heights, row_first, band_y, 1)
    fluid_cols = (
        jnp.arange(total_z, dtype=jnp.int32)[:, None, None] >= band_heights.T[None]
    ).astype(jnp.float32)
    bands = line_bands(padded_coef[:-1], padded_coef[1:], fluid_cols)
    row_ids = row_first + jnp.arange(band_y, dtype=jnp.int32)
    pressure = jnp.zeros_like(rhs_cols)
    for sweep_step in range(SWEEPS):
        for colour in (0, 1):
            pressure = column_sweep(pressure, rhs_cols, fluid_cols, bands, (row_ids + colour) % 2)
    pressure = lax.all_to_all(pressure, "gz", split_axis=0, concat_axis=1, tiled=True)
    padded = extended(pressure, (("gx", 2), ("gz", 0)), 1)
    padded = jnp.pad(padded, ((0, 0), (1, 1), (0, 0)))
    applied = (
        (4.0 + below_slab[:, None, None] + above_slab[:, None, None]) * pressure
        - below_slab[:, None, None] * padded[:-2, 1:-1, 1:-1]
        - above_slab[:, None, None] * padded[2:, 1:-1, 1:-1]
        - horizontal_sum(padded[1:-1])
    )
    residual = fluid_slab * (rhs_field - applied)
    coarse = (
        residual.reshape(slab_z // 2, 2, rows_y // 2, 2, width_x // 2, 2).sum(axis=(1, 3, 5))
        * 0.125
    )
    bundles = (
        coarse.reshape(slab_z // 2, rows_y // 2, 2, width_x // 4)
        .transpose(1, 2, 0, 3)
        .reshape(rows_y, -1)
    )
    outgoing = jnp.take(bundles, balance[0], axis=0)
    coarse_bundles = lax.all_to_all(outgoing, "gx", split_axis=0, concat_axis=0, tiled=True)
    return (pressure, coarse_bundles)


def solution(mesh):
    placed = (P("gz", None, "gx"), P("gx", None), P(), P("gx", None))
    return jax.shard_map(
        on_device,
        mesh=mesh,
        in_specs=placed,
        out_specs=(P("gz", None, "gx"), P("gx", "gz")),
        check_vma=False,
    )
```

profile of v0, /device:TPU:0, one launch (start us, length us, event | category | flops | bytes accessed | tf_op | source)
XLA Modules:
  0.0 331.7 jit_solution(15226701277065280224)
XLA Ops:
  0.7 4.8 %collective-permute-start = (f32[256,8,1]{0,1,2:T(8,128)S(1)}, f32[256,8,1]{0,1,2:T(8,128)S(1)}, u32[]{:S(2)}, u32[]{:S(2)}) collective-permute-start(f32[256,8,1]{0,1,2:T(8,128)S(1)} %broadcast.573), channel_id=1, source_target_pairs={{0,4},{4,8},{8,12},{12,16},{16,20},{20,24},{24,28},{1,5},{5,9},{9,... | collective-permute-start | bytes 24584 | tf_op jit(solution)/shard_map/ppermute | solution.py:17
  6.8 2.8 copy.136
  9.6 3.5 %all-to-all-start = ((f32[64,32,128]{2,0,1:T(8,128)}), f32[64,32,128]{2,0,1:T(8,128)S(1)}, u32[]{:S(2)}, u32[]{:S(2)}) async-start(f32[64,32,128]{2,0,1:T(8,128)} %copy.136), calls=%async_computation | async-start | bytes 2097152 | tf_op jit(solution)/shard_map/all_to_all | solution.py:102
  17.4 2.4 pad_maximum_fusion.49
  19.8 3.1 collective-permute-start.2
  24.6 3.0 all-to-all-done
  30.5 3.5 %fusion.5 = f32[256,8,128]{2,1,0:T(8,128)} fusion(f32[256,8,128]{2,1,0:T(8,128)S(1)} %copy-done.2, f32[256,8,1]{2,1,0:T(8,128)S(1)} %copy.140, f32[256,8,1]{2,1,0:T(8,128)S(1)} %copy.141, f32[256,1,130]{2,1,0:T(1,128)} %collective-permute-done.3, f32[256,1,130]{2,1,0:T(1,128)} %collective-permute-done.2, f32[4,64,8,128]{3,2,1,0:T(8,128)S(1)} %copy.138, ...), kind=kLoop, calls=%fused_computation.14 | loop fusion | flops 3145728 | bytes 3432448 | tf_op jit(solution)/shard_map/mul | solution.py:87
  35.8 2.2 fusion.35
  56.9 4.6 %collective-permute-start.4 = (f32[256,8,1]{0,1,2:T(8,128)S(1)}, f32[256,8,1]{0,1,2:T(8,128)S(1)}, u32[]{:S(2)}, u32[]{:S(2)}) collective-permute-start(f32[256,8,1]{0,1,2:T(8,128)S(1)} %copy.149), channel_id=1, source_target_pairs={{0,4},{4,8},{8,12},{12,16},{16,20},{20,24},{24,28},{1,5},{5,9},{9,... | collective-permute-start | bytes 24584 | tf_op jit(solution)/shard_map/ppermute | solution.py:17
  64.9 4.1 %collective-permute-done.5 = f32[256,8,1]{0,1,2:T(8,128)S(1)} collective-permute-done((f32[256,8,1]{0,1,2:T(8,128)S(1)}, f32[256,8,1]{0,1,2:T(8,128)S(1)}, u32[]{:S(2)}, u32[]{:S(2)}) %collective-permute-start.5) | collective-permute-done | bytes 8224 | tf_op jit(solution)/shard_map/ppermute | solution.py:19
  70.4 3.3 %pad_maximum_fusion.46 = (f32[256,1,130]{2,1,0:T(1,128)S(1)}, f32[256,1,130]{2,1,0:T(1,128)S(1)}) fusion(f32[256,8,1]{2,1,0:T(8,128)} %copy.152, f32[256,8,128]{2,1,0:T(8,128)S(1)} %broadcast_select_fusion, f32[256,8,1]{2,1,0:T(8,128)S(1)} %copy.150), kind=kLoop, calls=%fused_computation.228 | loop fusion | flops 133120 | bytes 1331200 | tf_op jit(solution)/shard_map/slice | solution.py:14
  79.4 3.0 fusion.26
  105.6 4.8 %collective-permute-start.8 = (f32[256,8,1]{0,1,2:T(8,128)S(1)}, f32[256,8,1]{0,1,2:T(8,128)S(1)}, u32[]{:S(2)}, u32[]{:S(2)}) collective-permute-start(f32[256,8,1]{0,1,2:T(8,128)S(1)} %copy.159), channel_id=1, source_target_pairs={{0,4},{4,8},{8,12},{12,16},{16,20},{20,24},{24,28},{1,5},{5,9},{9,... | collective-permute-start | bytes 24584 | tf_op jit(solution)/shard_map/ppermute | solution.py:17
  112.6 3.8 %collective-permute-done.9 = f32[256,8,1]{0,1,2:T(8,128)S(1)} collective-permute-done((f32[256,8,1]{0,1,2:T(8,128)S(1)}, f32[256,8,1]{0,1,2:T(8,128)S(1)}, u32[]{:S(2)}, u32[]{:S(2)}) %collective-permute-start.9) | collective-permute-done | bytes 8224 | tf_op jit(solution)/shard_map/ppermute | solution.py:19
  117.7 3.3 pad_maximum_fusion.43
  121.0 5.2 %collective-permute-start.10 = (f32[256,1,130]{2,1,0:T(1,128)S(1)}, f32[256,1,130]{2,1,0:T(1,128)S(1)}, u32[]{:S(2)}, u32[]{:S(2)}) collective-permute-start(f32[256,1,130]{2,1,0:T(1,128)S(1)} %get-tuple-element.77), channel_id=1, source_target_pairs={{0,1},{1,2},{2,3},{4,5},{5,6},{6,7},{8,9},{9,10},{10,11},{12,13},{... | collective-permute-start | bytes 399368 | tf_op jit(solution)/shard_map/ppermute | solution.py:17
  127.6 2.9 collective-permute-done.11
  130.5 3.0 fusion.21
  148.9 3.2 collective-permute-start.12
  154.2 3.8 %collective-permute-done.13 = f32[256,8,1]{0,1,2:T(8,128)S(1)} collective-permute-done((f32[256,8,1]{0,1,2:T(8,128)S(1)}, f32[256,8,1]{0,1,2:T(8,128)S(1)}, u32[]{:S(2)}, u32[]{:S(2)}) %collective-permute-start.13) | collective-permute-done | bytes 8224 | tf_op jit(solution)/shard_map/ppermute | solution.py:19
  159.3 3.3 pad_maximum_fusion.40
  162.7 5.5 %collective-permute-start.14 = (f32[256,1,130]{2,1,0:T(1,128)S(1)}, f32[256,1,130]{2,1,0:T(1,128)S(1)}, u32[]{:S(2)}, u32[]{:S(2)}) collective-permute-start(f32[256,1,130]{2,1,0:T(1,128)S(1)} %get-tuple-element.75), channel_id=1, source_target_pairs={{0,1},{1,2},{2,3},{4,5},{5,6},{6,7},{8,9},{9,10},{10,11},{12,13},{... | collective-permute-start | bytes 399368 | tf_op jit(solution)/shard_map/ppermute | solution.py:17
  169.5 2.6 collective-permute-done.15
  172.1 3.0 fusion.16
  185.8 6.0 %all-to-all-start.1 = ((f32[256,8,128]{2,1,0:T(8,128)}), f32[256,8,128]{2,1,0:T(8,128)S(1)}, u32[]{:S(2)}, u32[]{:S(2)}) async-start(f32[256,8,128]{2,1,0:T(8,128)} %broadcast_select_fusion.2), calls=%async_computation.1 | async-start | bytes 2097152 | tf_op jit(solution)/shard_map/all_to_all | solution.py:115
  193.1 13.2 %all-to-all-done.1 = f32[256,8,128]{2,1,0:T(8,128)S(1)} async-done(((f32[256,8,128]{2,1,0:T(8,128)}), f32[256,8,128]{2,1,0:T(8,128)S(1)}, u32[]{:S(2)}, u32[]{:S(2)}) %all-to-all-start.1) | async-done | bytes 1048608 | tf_op jit(solution)/shard_map/all_to_all | solution.py:115
  207.4 4.8 %collective-permute-start.16 = (f32[64,32,1]{0,1,2:T(8,128)S(1)}, f32[64,32,1]{0,1,2:T(8,128)S(1)}, u32[]{:S(2)}, u32[]{:S(2)}) collective-permute-start(f32[64,32,1]{0,1,2:T(8,128)S(1)} %copy.181), channel_id=1, source_target_pairs={{0,4},{4,8},{8,12},{12,16},{16,20},{20,24},{24,28},{1,5},{5,9},{9,... | collective-permute-start | bytes 24584 | tf_op jit(solution)/shard_map/ppermute | solution.py:17
  215.5 3.0 collective-permute-done.17
  225.2 3.6 %fusion.8 = f32[64,32,128]{2,1,0:T(8,128)} fusion(f32[64,32,128]{2,1,0:T(8,128)S(1)} %copy-done.83, f32[66,34,130]{2,1,0:T(8,128)S(1)} %select_maximum_fusion, f32[64,32,1]{2,1,0:T(8,128)S(1)} %copy.184, f32[64,32,128]{2,1,0:T(8,128)S(1)} %bitcast.140, f32[64,32,1]{2,1,0:T(8,128)S(1)} %copy.183, f32[1,32,130]{2,1,0:T(8,128)S(1)} %collective-permute-done.19, ...), kind=kLoop, calls=%fused_computation.18 | loop fusion | flops 5242880 | bytes 5309952 | tf_op jit(solution)/shard_map/mul | solution.py:124
  228.8 69.1 %reshape.197 = f32[32,2,16,2,64,2]{5,4,3,2,1,0:T(8,128)} reshape(f32[64,32,128]{2,1,0:T(8,128)} %fusion.8) | data formatting | bytes 2097152 | tf_op jit(solution)/shard_map/reshape | solution.py:126
  297.9 20.8 %reduce_sum.9 = f32[32,16,64]{2,1,0:T(8,128)S(1)} reduce(f32[32,2,16,2,64,2]{5,4,3,2,1,0:T(8,128)} %reshape.197, f32[]{:T(128)} %constant.91.clone.1), dimensions={1,3,5}, to_apply=%region_0.1 | reduce | flops 229376 | bytes 1179652 | tf_op jit(solution)/shard_map/reduce_sum | solution.py:126
  320.4 10.4 %all_to_all.45 = f32[8,4,1024]{2,1,0:T(4,128)S(1)} all-to-all(f32[8,4,1024]{2,1,0:T(4,128)S(1)} %broadcast_select_fusion.4), channel_id=1, replica_groups=mesh['gx'=8,'gz'=4] {'gx'}, dimensions={0} | all-to-all | bytes 262144 | tf_op jit(solution)/shard_map/all_to_all | solution.py:135
  (441 shorter events, 113.1 us)
Async XLA Ops:
  0.6 12.5 %copy-start.100 = (s32[128,32]{0,1:T(8,128)S(1)}, s32[128,32]{0,1:T(8,128)}, u32[]{:S(2)}) copy-start(s32[128,32]{0,1:T(8,128)} %param.5) | copy-start | bytes 49156
  0.6 12.7 %copy-start.101 = (f32[256]{0:T(256)S(1)}, f32[256]{0:T(256)}, u32[]{:S(2)}) copy-start(f32[256]{0:T(256)} %param.6) | copy-start | bytes 3076
  0.7 14.8 %collective-permute-start = (f32[256,8,1]{0,1,2:T(8,128)S(1)}, f32[256,8,1]{0,1,2:T(8,128)S(1)}, u32[]{:S(2)}, u32[]{:S(2)}) collective-permute-start(f32[256,8,1]{0,1,2:T(8,128)S(1)} %broadcast.573), channel_id=1, source_target_pairs={{0,4},{4,8},{8,12},{12,16},{16,20},{20,24},{24,28},{1,5},{5,9},{9,... | collective-permute-start | bytes 24584 | tf_op jit(solution)/shard_map/ppermute | solution.py:17
  5.5 10.4 %collective-permute-start.1 = (f32[256,8,1]{0,1,2:T(8,128)S(1)}, f32[256,8,1]{0,1,2:T(8,128)S(1)}, u32[]{:S(2)}, u32[]{:S(2)}) collective-permute-start(f32[256,8,1]{0,1,2:T(8,128)S(1)} %broadcast.573), channel_id=1, source_target_pairs={{4,0},{8,4},{12,8},{16,12},{20,16},{24,20},{28,24},{5,1},{9,5},{13... | collective-permute-start | bytes 24584 | tf_op jit(solution)/shard_map/ppermute | solution.py:19
  9.6 18.0 %all-to-all-start = ((f32[64,32,128]{2,0,1:T(8,128)}), f32[64,32,128]{2,0,1:T(8,128)S(1)}, u32[]{:S(2)}, u32[]{:S(2)}) async-start(f32[64,32,128]{2,0,1:T(8,128)} %copy.136), calls=%async_computation | async-start | bytes 2097152 | tf_op jit(solution)/shard_map/all_to_all | solution.py:102
  19.8 10.7 %collective-permute-start.2 = (f32[256,1,130]{2,1,0:T(1,128)}, f32[256,1,130]{2,1,0:T(1,128)}, u32[]{:S(2)}, u32[]{:S(2)}) collective-permute-start(f32[256,1,130]{2,1,0:T(1,128)} %get-tuple-element.81), channel_id=1, source_target_pairs={{0,1},{1,2},{2,3},{4,5},{5,6},{6,7},{8,9},{9,10},{10,11},{12,13},{... | collective-permute-start | bytes 399368 | tf_op jit(solution)/shard_map/ppermute | solution.py:17
  22.9 7.6 %collective-permute-start.3 = (f32[256,1,130]{2,1,0:T(1,128)S(1)}, f32[256,1,130]{2,1,0:T(1,128)}, u32[]{:S(2)}, u32[]{:S(2)}) collective-permute-start(f32[256,1,130]{2,1,0:T(1,128)S(1)} %get-tuple-element.82), channel_id=1, source_target_pairs={{1,0},{2,1},{3,2},{5,4},{6,5},{7,6},{9,8},{10,9},{11,10},{13,12},{... | collective-permute-start | bytes 399368 | tf_op jit(solution)/shard_map/ppermute | solution.py:19
  56.9 7.6 %collective-permute-start.4 = (f32[256,8,1]{0,1,2:T(8,128)S(1)}, f32[256,8,1]{0,1,2:T(8,128)S(1)}, u32[]{:S(2)}, u32[]{:S(2)}) collective-permute-start(f32[256,8,1]{0,1,2:T(8,128)S(1)} %copy.149), channel_id=1, source_target_pairs={{0,4},{4,8},{8,12},{12,16},{16,20},{20,24},{24,28},{1,5},{5,9},{9,... | collective-permute-start | bytes 24584 | tf_op jit(solution)/shard_map/ppermute | solution.py:17
  63.0 6.0 %collective-permute-start.5 = (f32[256,8,1]{0,1,2:T(8,128)S(1)}, f32[256,8,1]{0,1,2:T(8,128)S(1)}, u32[]{:S(2)}, u32[]{:S(2)}) collective-permute-start(f32[256,8,1]{0,1,2:T(8,128)S(1)} %copy.151), channel_id=1, source_target_pairs={{4,0},{8,4},{12,8},{16,12},{20,16},{24,20},{28,24},{5,1},{9,5},{13... | collective-permute-start | bytes 24584 | tf_op jit(solution)/shard_map/ppermute | solution.py:19
  70.4 6.7 %copy-start.50 = (f32[256,8,64]{0,1,2:T(8,128)S(1)}, f32[256,8,64]{0,1,2:T(8,128)}, u32[]{:S(2)}) copy-start(f32[256,8,64]{0,1,2:T(8,128)} %get-tuple-element.89) | copy-start | bytes 1572868
  70.4 9.0 %copy-start.3 = (f32[256,8,1]{2,1,0:T(8,128)S(1)}, f32[256,8,1]{2,1,0:T(8,128)}, u32[]{:S(2)}) copy-start(f32[256,8,1]{2,1,0:T(8,128)} %copy.152) | copy-start | bytes 24580
  73.7 4.5 %collective-permute-start.6 = (f32[256,1,130]{2,1,0:T(1,128)S(1)}, f32[256,1,130]{2,1,0:T(1,128)S(1)}, u32[]{:S(2)}, u32[]{:S(2)}) collective-permute-start(f32[256,1,130]{2,1,0:T(1,128)S(1)} %get-tuple-element.79), channel_id=1, source_target_pairs={{0,1},{1,2},{2,3},{4,5},{5,6},{6,7},{8,9},{9,10},{10,11},{12,13},{... | collective-permute-start | bytes 399368 | tf_op jit(solution)/shard_map/ppermute | solution.py:17
  75.8 3.6 %collective-permute-start.7 = (f32[256,1,130]{2,1,0:T(1,128)S(1)}, f32[256,1,130]{2,1,0:T(1,128)S(1)}, u32[]{:S(2)}, u32[]{:S(2)}) collective-permute-start(f32[256,1,130]{2,1,0:T(1,128)S(1)} %get-tuple-element.80), channel_id=1, source_target_pairs={{1,0},{2,1},{3,2},{5,4},{6,5},{7,6},{9,8},{10,9},{11,10},{13,12},{... | collective-permute-start | bytes 399368 | tf_op jit(solution)/shard_map/ppermute | solution.py:19
  82.4 2.2 copy-start.7
  105.6 6.5 %collective-permute-start.8 = (f32[256,8,1]{0,1,2:T(8,128)S(1)}, f32[256,8,1]{0,1,2:T(8,128)S(1)}, u32[]{:S(2)}, u32[]{:S(2)}) collective-permute-start(f32[256,8,1]{0,1,2:T(8,128)S(1)} %copy.159), channel_id=1, source_target_pairs={{0,4},{4,8},{8,12},{12,16},{16,20},{20,24},{24,28},{1,5},{5,9},{9,... | collective-permute-start | bytes 24584 | tf_op jit(solution)/shard_map/ppermute | solution.py:17
  110.8 5.5 %collective-permute-start.9 = (f32[256,8,1]{0,1,2:T(8,128)S(1)}, f32[256,8,1]{0,1,2:T(8,128)S(1)}, u32[]{:S(2)}, u32[]{:S(2)}) collective-permute-start(f32[256,8,1]{0,1,2:T(8,128)S(1)} %copy.161), channel_id=1, source_target_pairs={{4,0},{8,4},{12,8},{16,12},{20,16},{24,20},{28,24},{5,1},{9,5},{13... | collective-permute-start | bytes 24584 | tf_op jit(solution)/shard_map/ppermute | solution.py:19
  117.7 12.8 %copy-start.5 = (f32[256,8,1]{2,1,0:T(8,128)S(1)}, f32[256,8,1]{2,1,0:T(8,128)}, u32[]{:S(2)}) copy-start(f32[256,8,1]{2,1,0:T(8,128)} %copy.162) | copy-start | bytes 24580
  121.0 6.6 %collective-permute-start.10 = (f32[256,1,130]{2,1,0:T(1,128)S(1)}, f32[256,1,130]{2,1,0:T(1,128)S(1)}, u32[]{:S(2)}, u32[]{:S(2)}) collective-permute-start(f32[256,1,130]{2,1,0:T(1,128)S(1)} %get-tuple-element.77), channel_id=1, source_target_pairs={{0,1},{1,2},{2,3},{4,5},{5,6},{6,7},{8,9},{9,10},{10,11},{12,13},{... | collective-permute-start | bytes 399368 | tf_op jit(solution)/shard_map/ppermute | solution.py:17
  126.3 4.2 %collective-permute-start.11 = (f32[256,1,130]{2,1,0:T(1,128)S(1)}, f32[256,1,130]{2,1,0:T(1,128)S(1)}, u32[]{:S(2)}, u32[]{:S(2)}) collective-permute-start(f32[256,1,130]{2,1,0:T(1,128)S(1)} %get-tuple-element.78), channel_id=1, source_target_pairs={{1,0},{2,1},{3,2},{5,4},{6,5},{7,6},{9,8},{10,9},{11,10},{13,12},{... | collective-permute-start | bytes 399368 | tf_op jit(solution)/shard_map/ppermute | solution.py:19
  148.9 4.8 %collective-permute-start.12 = (f32[256,8,1]{0,1,2:T(8,128)S(1)}, f32[256,8,1]{0,1,2:T(8,128)S(1)}, u32[]{:S(2)}, u32[]{:S(2)}) collective-permute-start(f32[256,8,1]{0,1,2:T(8,128)S(1)} %copy.169), channel_id=1, source_target_pairs={{0,4},{4,8},{8,12},{12,16},{16,20},{20,24},{24,28},{1,5},{5,9},{9,... | collective-permute-start | bytes 24584 | tf_op jit(solution)/shard_map/ppermute | solution.py:17
  152.4 5.6 %collective-permute-start.13 = (f32[256,8,1]{0,1,2:T(8,128)S(1)}, f32[256,8,1]{0,1,2:T(8,128)S(1)}, u32[]{:S(2)}, u32[]{:S(2)}) collective-permute-start(f32[256,8,1]{0,1,2:T(8,128)S(1)} %copy.171), channel_id=1, source_target_pairs={{4,0},{8,4},{12,8},{16,12},{20,16},{24,20},{28,24},{5,1},{9,5},{13... | collective-permute-start | bytes 24584 | tf_op jit(solution)/shard_map/ppermute | solution.py:19
  159.3 12.8 %copy-start.4 = (f32[256,8,1]{2,1,0:T(8,128)S(1)}, f32[256,8,1]{2,1,0:T(8,128)}, u32[]{:S(2)}) copy-start(f32[256,8,1]{2,1,0:T(8,128)} %copy.172) | copy-start | bytes 24580
  162.7 6.8 %collective-permute-start.14 = (f32[256,1,130]{2,1,0:T(1,128)S(1)}, f32[256,1,130]{2,1,0:T(1,128)S(1)}, u32[]{:S(2)}, u32[]{:S(2)}) collective-permute-start(f32[256,1,130]{2,1,0:T(1,128)S(1)} %get-tuple-element.75), channel_id=1, source_target_pairs={{0,1},{1,2},{2,3},{4,5},{5,6},{6,7},{8,9},{9,10},{10,11},{12,13},{... | collective-permute-start | bytes 399368 | tf_op jit(solution)/shard_map/ppermute | solution.py:17
  168.2 3.9 %collective-permute-start.15 = (f32[256,1,130]{2,1,0:T(1,128)S(1)}, f32[256,1,130]{2,1,0:T(1,128)S(1)}, u32[]{:S(2)}, u32[]{:S(2)}) collective-permute-start(f32[256,1,130]{2,1,0:T(1,128)S(1)} %get-tuple-element.76), channel_id=1, source_target_pairs={{1,0},{2,1},{3,2},{5,4},{6,5},{7,6},{9,8},{10,9},{11,10},{13,12},{... | collective-permute-start | bytes 399368 | tf_op jit(solution)/shard_map/ppermute | solution.py:19
  184.7 7.6 %copy-start.102 = (s32[1,32]{1,0:T(1,128)S(1)}, s32[1,32]{1,0:T(1,128)}, u32[]{:S(2)}) copy-start(s32[1,32]{1,0:T(1,128)} %param.7) | copy-start | bytes 388
  185.8 20.5 %all-to-all-start.1 = ((f32[256,8,128]{2,1,0:T(8,128)}), f32[256,8,128]{2,1,0:T(8,128)S(1)}, u32[]{:S(2)}, u32[]{:S(2)}) async-start(f32[256,8,128]{2,1,0:T(8,128)} %broadcast_select_fusion.2), calls=%async_computation.1 | async-start | bytes 2097152 | tf_op jit(solution)/shard_map/all_to_all | solution.py:115
  206.4 18.7 %copy-start = (f32[64,4,8,128]{3,2,1,0:T(8,128)}, f32[64,4,8,128]{3,2,1,0:T(8,128)S(1)}, u32[]{:S(2)}) copy-start(f32[64,4,8,128]{3,2,1,0:T(8,128)S(1)} %copy.197) | copy-start | bytes 3145732
  207.4 7.1 %collective-permute-start.16 = (f32[64,32,1]{0,1,2:T(8,128)S(1)}, f32[64,32,1]{0,1,2:T(8,128)S(1)}, u32[]{:S(2)}, u32[]{:S(2)}) collective-permute-start(f32[64,32,1]{0,1,2:T(8,128)S(1)} %copy.181), channel_id=1, source_target_pairs={{0,4},{4,8},{8,12},{12,16},{16,20},{20,24},{24,28},{1,5},{5,9},{9,... | collective-permute-start | bytes 24584 | tf_op jit(solution)/shard_map/ppermute | solution.py:17
  212.9 5.6 %collective-permute-start.17 = (f32[64,32,1]{0,1,2:T(8,128)S(1)}, f32[64,32,1]{0,1,2:T(8,128)S(1)}, u32[]{:S(2)}, u32[]{:S(2)}) collective-permute-start(f32[64,32,1]{0,1,2:T(8,128)S(1)} %copy.182), channel_id=1, source_target_pairs={{4,0},{8,4},{12,8},{16,12},{20,16},{24,20},{28,24},{5,1},{9,5},{13... | collective-permute-start | bytes 24584 | tf_op jit(solution)/shard_map/ppermute | solution.py:19
  219.6 2.6 collective-permute-start.18
  220.9 3.1 collective-permute-start.19
  222.2 2.9 copy-start.83
  (93 other events, 114.5 us)
where the time goes:
time: 337 us; the launch traced here: 332 us
  local copies, waits for them, and re-layouts  141 us (42%)
  other arithmetic  75.7 us (22%)
  starting transfers between devices  62.3 us (18%)
  waiting for transfers between devices  39.3 us (12%)
  blocking collectives  10.4 us (3%)
    reshape x1, local copies, waits for them, and re-layouts, on_device(): residual.reshape(slab_z // 2, 2, rows_y // 2, 2, width_x // 2, 2)  69.1 us
    ppermute x10, starting transfers between devices, extended(): lax.ppermute(tail, axis, [(i, (i + 1) % count) for i in range(ends)])  39.4 us
    ppermute x10, waiting for transfers between devices, extended(): lax.ppermute(head, axis, [((i + 1) % count, i) for i in range(ends)])  23.1 us
    reduce_sum x1, other arithmetic, on_device(): residual.reshape(slab_z // 2, 2, rows_y // 2, 2, width_x // 2, 2)  20.8 us
    unnamed x208, local copies, waits for them, and re-layouts  19.3 us
    ppermute x10, starting transfers between devices, extended(): lax.ppermute(head, axis, [((i + 1) % count, i) for i in range(ends)])  13.3 us
    all_to_all x1, waiting for transfers between devices, on_device(): lax.all_to_all(pressure, 'gz', split_axis=0, concat_axis=1, tiled=True)  13.2 us
    mul x4, other arithmetic, column_sweep(): right_side = fluid_cols * (rhs_cols + horizontal_sum(padded))  12.5 us
  transfers between devices with their start and end apart: 22, of which 10 were waited for; matrix products, arithmetic and copies ran while one was open for 6% of the time, Pallas kernels for 0%

commit v1 on v0

v1 whole, which is shorter than its diff:
```python
import functools

import jax
import jax.numpy as jnp
from jax import lax
from jax.experimental import pallas as pl
from jax.experimental.pallas import tpu as pltpu
from jax.sharding import PartitionSpec as P

SWEEPS = 2
SOLVES = 2 * SWEEPS
UNROLL = 4
MESH = pl.DeviceIdType.MESH


def relax_kernel(
    n_gz,
    n_gx,
    rhs_ref,
    heights_ref,
    coef_ref,
    balance_ref,
    pool_ref,
    p_ref,
    out_ref,
    side_inv,
    low_inv,
    upper,
    low_spike,
    up_spike,
    local,
    delta,
    ends,
    spikes,
    reduced,
    firsts,
    lasts,
    halo_out,
    halo_in,
    pooled,
    bundles,
    outgoing,
    arrived,
    ends_send,
    ends_recv,
    spikes_send,
    spikes_recv,
    halo_send,
    halo_recv,
    tail_send,
    tail_recv,
):
    levels, rows, width = rhs_ref.shape
    total_z = coef_ref.shape[0]
    gz = lax.axis_index("gz")
    gx = lax.axis_index("gx")
    first_level = gz * levels

    barrier = pltpu.get_barrier_semaphore()
    for o in range(1, n_gz):
        pl.semaphore_signal(
            barrier, inc=1, device_id=(gx, lax.rem(gz + o, n_gz)), device_id_type=MESH
        )
    for o in range(1, n_gx):
        pl.semaphore_signal(
            barrier, inc=1, device_id=(lax.rem(gx + o, n_gx), gz), device_id_type=MESH
        )

    zero = jnp.zeros((rows, width), jnp.float32)
    one = jnp.ones((rows, width), jnp.float32)
    lane = lax.broadcasted_iota(jnp.int32, (rows, width), 1)
    row = lax.broadcasted_iota(jnp.int32, (rows, width), 0)
    parity = lax.rem(lane + row + gx * width, 2)
    at_left = lane == 0
    at_right = lane == width - 1
    at_top = row == 0
    at_bottom = row == rows - 1

    @pl.when(gx == 0)
    def _():
        for t in range(SOLVES):
            halo_in[t, 0] = zero

    @pl.when(gx == n_gx - 1)
    def _():
        for t in range(SOLVES):
            halo_in[t, 1] = zero

    def fluid_at(k):
        return (first_level + k >= heights_ref[...]).astype(jnp.float32)

    def factor(k, carry):
        up_before, d_before, spike_before = carry
        z = first_level + k
        below = coef_ref[z]
        above = jnp.where(z + 1 < total_z, coef_ref[jnp.minimum(z + 1, total_z - 1)], 0.0)
        fluid = fluid_at(k)
        low = -below * fluid
        centre = fluid * (4.0 + below + above) + (1.0 - fluid)
        inverse = 1.0 / (centre - low * up_before)
        up = -above * fluid * inverse
        low = low * inverse
        scale = fluid * inverse
        d = rhs_ref[k] * scale - low * d_before
        spike = -low * spike_before
        upper[k] = up
        low_inv[k] = low
        side_inv[k] = scale
        local[k] = d
        low_spike[k] = spike
        return up, d, spike

    def factor_back(i, carry):
        k = levels - 1 - i
        g_after, low_after, up_after = carry
        up = upper[k]
        g = local[k] - up * g_after
        low = low_spike[k] - up * low_after
        high = -up * up_after
        local[k] = g
        low_spike[k] = low
        up_spike[k] = high
        return g, low, high

    def around(cells, left_edge, right_edge):
        left = jnp.where(at_left, left_edge, pltpu.roll(cells, 1, 1))
        right = jnp.where(at_right, right_edge, pltpu.roll(cells, width - 1, 1))
        up = jnp.where(at_top, 0.0, pltpu.roll(cells, 1, 0))
        down = jnp.where(at_bottom, 0.0, pltpu.roll(cells, rows - 1, 0))
        return (left + right) + (up + down)

    def next_edge(edge):
        return pltpu.roll(edge, width - 1, 1)

    def forward(k, carry):
        d_before, left_edge, right_edge = carry
        side = rhs_ref[k] + around(p_ref[k], left_edge, right_edge)
        d = side * side_inv[k] - low_inv[k] * d_before
        local[k] = d
        return d, next_edge(left_edge), next_edge(right_edge)

    def backward(i, g_after):
        k = levels - 1 - i
        g = local[k] - upper[k] * g_after
        local[k] = g
        return g

    def halo_copies(t):
        to_right = pltpu.make_async_remote_copy(
            src_ref=halo_out.at[t, 0],
            dst_ref=halo_in.at[t, 0],
            send_sem=halo_send.at[t, 0],
            recv_sem=halo_recv.at[t, 0],
            device_id=(lax.rem(gx + 1, n_gx), gz),
            device_id_type=MESH,
        )
        to_left = pltpu.make_async_remote_copy(
            src_ref=halo_out.at[t, 1],
            dst_ref=halo_in.at[t, 1],
            send_sem=halo_send.at[t, 1],
            recv_sem=halo_recv.at[t, 1],
            device_id=(lax.rem(gx + n_gx - 1, n_gx), gz),
            device_id_type=MESH,
        )
        return to_right, to_left

    def start_halo(t):
        to_right, to_left = halo_copies(t)

        @pl.when(gx < n_gx - 1)
        def _():
            to_right.start()

        @pl.when(gx > 0)
        def _():
            to_left.start()

    def finish_halo(t):
        to_right, to_left = halo_copies(t)

        @pl.when(gx > 0)
        def _():
            to_left.wait_send()
            to_right.wait_recv()

        @pl.when(gx < n_gx - 1)
        def _():
            to_right.wait_send()
            to_left.wait_recv()

        left_edge = pltpu.roll(halo_in[t, 0], levels % width, 1)
        right_edge = pltpu.roll(halo_in[t, 1], (levels - 2) % width, 1)
        return left_edge, right_edge

    def column_copy(ref, send, recv, o):
        return pltpu.make_async_remote_copy(
            src_ref=ref.at[gz],
            dst_ref=ref.at[gz],
            send_sem=send.at[o - 1],
            recv_sem=recv.at[o - 1],
            device_id=(gx, lax.rem(gz + o, n_gz)),
            device_id_type=MESH,
        )

    for t in range(SOLVES):
        colour = t % 2
        if t == 0:
            lax.fori_loop(0, levels, factor, (zero, zero, one), unroll=UNROLL)
            d_last = local[levels - 1]
            g, low, high = lax.fori_loop(0, levels, factor_back, (zero, zero, one), unroll=UNROLL)
            spikes[gz, 0] = low
            spikes[gz, 1] = low_spike[levels - 1]
            spikes[gz, 2] = high
            spikes[gz, 3] = up_spike[levels - 1]
        else:
            left_edge, right_edge = finish_halo(t - 1)
            d_last, _, _ = lax.fori_loop(
                0, levels, forward, (zero, left_edge, right_edge), unroll=UNROLL
            )
            g = lax.fori_loop(0, levels, backward, zero, unroll=UNROLL)
        ends[t, gz, 0] = g
        ends[t, gz, 1] = d_last
        copies = [
            column_copy(ends.at[t], ends_send.at[t], ends_recv.at[t], o) for o in range(1, n_gz)
        ]
        if t == 0:
            copies += [column_copy(spikes, spikes_send, spikes_recv, o) for o in range(1, n_gz)]
            pl.semaphore_wait(barrier, n_gz + n_gx - 2)
        for copy in copies:
            copy.start()
        for copy in copies:
            copy.wait()

        if t == 0:
            beta = zero
            for s in range(n_gz):
                inverse = 1.0 / (1.0 - spikes[s, 0] * beta)
                reduced[s, 0] = beta
                reduced[s, 1] = inverse
                reduced[s, 2] = spikes[s, 2] * inverse
                beta = spikes[s, 3] + spikes[s, 1] * beta * reduced[s, 2]
                reduced[s, 3] = beta
        alpha = zero
        heads, tails = [], []
        for s in range(n_gz):
            head = (ends[t, s, 0] + spikes[s, 0] * alpha) * reduced[s, 1]
            alpha = ends[t, s, 1] + spikes[s, 1] * (alpha + reduced[s, 0] * head)
            heads.append(head)
            tails.append(alpha)
        after = zero
        firsts[n_gz] = zero
        lasts[0] = zero
        for s in reversed(range(n_gz)):
            lasts[s + 1] = tails[s] + reduced[s, 3] * after
            after = heads[s] + reduced[s, 2] * after
            firsts[s] = after
        below_value = lasts[gz]
        above_value = firsts[gz + 1]

        def correct(k, carry):
            to_right, to_left = carry
            value = local[k] + low_spike[k] * below_value + up_spike[k] * above_value
            before = zero if t == 0 else p_ref[k]
            cells = jnp.where(parity == colour, value, before)
            p_ref[k] = cells
            if t == SOLVES - 1:
                cells = cells - before
                delta[k] = cells
            to_right = jnp.where(at_right, cells, next_edge(to_right))
            to_left = jnp.where(at_left, cells, next_edge(to_left))
            return to_right, to_left

        to_right, to_left = lax.fori_loop(0, levels, correct, (zero, zero), unroll=UNROLL)
        halo_out[t, 0] = to_right
        halo_out[t, 1] = to_left
        start_halo(t)

    def coarsen(i, carry):
        left_edge, right_edge = carry
        total = zero
        for j in range(2):
            k = 2 * i + j
            total += fluid_at(k) * around(delta[k], left_edge, right_edge)
            left_edge, right_edge = next_edge(left_edge), next_edge(right_edge)
        local[i] = total
        return left_edge, right_edge

    lax.fori_loop(0, levels // 2, coarsen, finish_halo(SOLVES - 1), unroll=2)

    half = rows // 2
    per_row = width // (width // 4)
    chunks = levels // 2 // per_row
    for i in range(levels // 2):
        c, part = i // per_row, i % per_row
        pooled[c * half : (c + 1) * half, part * width : (part + 1) * width] = (
            local[i, pl.ds(0, half, 2), :] + local[i, pl.ds(1, half, 2), :]
        )
    packed = jnp.dot(
        pooled[...],
        pool_ref[...],
        preferred_element_type=jnp.float32,
        precision=lax.Precision.HIGHEST,
    )
    for c in range(chunks):
        for h in range(2):
            bundles[h * half : (h + 1) * half, c, :] = packed[
                c * half : (c + 1) * half, h * width : (h + 1) * width
            ]
    share = rows // n_gx
    for j in range(rows):
        b = balance_ref[0, j]
        outgoing[j] = bundles[(b & 1) * half + (b >> 1)]
    copies = []
    for o in range(1, n_gx):
        owner = lax.rem(gx + o, n_gx)
        copies.append(
            pltpu.make_async_remote_copy(
                src_ref=outgoing.at[pl.ds(owner * share, share)],
                dst_ref=arrived.at[pl.ds(gx * share, share)],
                send_sem=tail_send.at[o - 1],
                recv_sem=tail_recv.at[o - 1],
                device_id=(owner, gz),
                device_id_type=MESH,
            )
        )
    for copy in copies:
        copy.start()
    arrived[pl.ds(gx * share, share)] = outgoing[pl.ds(gx * share, share)]
    for copy in copies:
        copy.wait()
    for c in range(chunks):
        out_ref[:, c * width : (c + 1) * width] = arrived[:, c, :]


def on_device(n_gz, n_gx, rhs_field, heights, vert_coef, balance):
    levels, rows, width = rhs_field.shape
    per_row = 4
    chunks = levels // 2 // per_row
    spot = jnp.arange(per_row * width, dtype=jnp.int32)[:, None]
    target = jnp.arange(2 * width, dtype=jnp.int32)[None, :]
    quarter = width // 4
    coarse_x = (spot % width) // 2
    pool = jnp.where(
        (target // width == coarse_x // quarter)
        & (target % width == (spot // width) * quarter + coarse_x % quarter),
        0.125,
        0.0,
    ).astype(jnp.float32)
    vmem = pl.BlockSpec(memory_space=pltpu.VMEM)
    smem = pl.BlockSpec(memory_space=pltpu.SMEM)
    slab = pltpu.VMEM((levels, rows, width), jnp.float32)
    plane = (rows, width)

    def planes(*lead):
        return pltpu.VMEM(lead + plane, jnp.float32)

    def sems(*lead):
        return pltpu.SemaphoreType.DMA(lead)

    pressure, coarse = pl.pallas_call(
        functools.partial(relax_kernel, n_gz, n_gx),
        out_shape=(
            jax.ShapeDtypeStruct(rhs_field.shape, jnp.float32),
            jax.ShapeDtypeStruct((rows, chunks * width), jnp.float32),
        ),
        in_specs=[vmem, vmem, smem, smem, vmem],
        out_specs=(vmem, vmem),
        scratch_shapes=[slab] * 7
        + [
            planes(SOLVES, n_gz, 2),
            planes(n_gz, 4),
            planes(n_gz, 4),
            planes(n_gz + 1),
            planes(n_gz + 1),
            planes(SOLVES, 2),
            planes(SOLVES, 2),
            pltpu.VMEM((chunks * rows // 2, per_row * width), jnp.float32),
            pltpu.VMEM((rows, chunks, width), jnp.float32),
            pltpu.VMEM((rows, chunks, width), jnp.float32),
            pltpu.VMEM((rows, chunks, width), jnp.float32),
            sems(SOLVES, n_gz - 1),
            sems(SOLVES, n_gz - 1),
            sems(n_gz - 1),
            sems(n_gz - 1),
            sems(SOLVES, 2),
            sems(SOLVES, 2),
            sems(n_gx - 1),
            sems(n_gx - 1),
        ],
        compiler_params=pltpu.CompilerParams(
            collective_id=0, has_side_effects=True, vmem_limit_bytes=32 * 1024 * 1024
        ),
    )(rhs_field, heights.T, vert_coef, balance, pool)
    return pressure, coarse


def solution(mesh):
    placed = (P("gz", None, "gx"), P("gx", None), P(), P("gx", None))
    return jax.shard_map(
        functools.partial(on_device, mesh.shape["gz"], mesh.shape["gx"]),
        mesh=mesh,
        in_specs=placed,
        out_specs=(P("gz", None, "gx"), P("gx", "gz")),
        check_vma=False,
    )
```

time: 337 us -> 79.7 us (0.24); the launches traced: 332 us -> 79.4 us
  local copies, waits for them, and re-layouts: 141 us -> 3.34 us
  other arithmetic: 75.7 us -> 0.22 us
  Pallas kernels: 0 us -> 75.2 us
  starting transfers between devices: 62.3 us -> 0 us
  waiting for transfers between devices: 39.3 us -> 0 us
  blocking collectives: 10.4 us -> 0 us
    pallas_call x0 -> x1, Pallas kernels: none -> 75.2 us  [on_device(): pl.pallas_call(functools.partial(relax_kernel, n_gz, n_gx), out_shape=(ja...]
    reshape x2 -> x0, local copies, waits for them, and re-layouts: 69.4 us -> none  [the longest x1 69.1 us: on_device(): residual.reshape(slab_z // 2, 2, rows_y // 2, 2, width_x // 2, 2)]
    ppermute x20 -> x0, starting transfers between devices: 52.7 us -> none  [the longest x10 39.4 us: extended(): lax.ppermute(tail, axis, [(i, (i + 1) % count) for i in range(ends)])]
    slice x92 -> x0, local copies, waits for them, and re-layouts: 28.2 us -> none  [the longest x8 9.86 us: extended(): lax.slice_in_dim(cells, cells.shape[dim] - width, cells.shape[dim], axis=...]
    ppermute x20 -> x0, waiting for transfers between devices: 23.1 us -> none  [the longest x10 23.1 us: extended(): lax.ppermute(head, axis, [((i + 1) % count, i) for i in range(ends)])]
    reduce_sum x1 -> x0, other arithmetic: 20.8 us -> none  [on_device(): residual.reshape(slab_z // 2, 2, rows_y // 2, 2, width_x // 2, 2)]
    mul x12 -> x0, other arithmetic: 17.9 us -> none  [the longest x4 12.5 us: column_sweep(): right_side = fluid_cols * (rhs_cols + horizontal_sum(padded))]
    all_to_all x2 -> x0, waiting for transfers between devices: 16.2 us -> none  [the longest x1 13.2 us: on_device(): lax.all_to_all(pressure, 'gz', split_axis=0, concat_axis=1, tiled=True)]
  transfers between devices with their start and end apart: 22 -> 0, of which waited for: 10 -> 0; matrix products, arithmetic and copies ran while one was open for 6% -> 0% of each run, Pallas kernels for 0% -> 0%
where the time goes in v1:
time: 79.7 us; the launch traced here: 79.4 us
  Pallas kernels  75.2 us (94%)
  local copies, waits for them, and re-layouts  3.34 us (4%)
    pallas_call x1, Pallas kernels, on_device(): pl.pallas_call(functools.partial(relax_kernel, n_gz, n_gx), out_shape=(ja...  75.2 us
    unnamed x10, local copies, waits for them, and re-layouts  3.34 us

profile of v1, /device:TPU:0, one launch (start us, length us, event | category | flops | bytes accessed | tf_op | source)
XLA Modules:
  0.0 79.4 jit_solution(4164180590236933667)
XLA Ops:
  0.7 0.0 copy-start.1
  0.7 0.0 copy-start.2
  0.7 0.0 copy-start.3
  0.7 0.2 and_select_fusion.pool_ref
  0.9 0.5 copy-done.1
  1.4 0.0 copy-done.2
  1.4 0.0 copy-done.3
  1.4 0.0 copy-start
  1.4 1.2 %copy-done = f32[64,32,128]{2,1,0:T(8,128)S(1)} copy-done((f32[64,32,128]{2,1,0:T(8,128)S(1)}, f32[64,32,128]{2,1,0:T(8,128)}, u32[]{:S(2)}) %copy-start) | copy-done | bytes 1048600
  2.6 75.2 %shard_map.59 = (f32[64,32,128]{2,1,0:T(8,128)S(1)}, f32[32,1024]{1,0:T(8,128)S(1)}) custom-call(f32[64,32,128]{2,1,0:T(8,128)S(1)} %copy-done, s32[32,128]{1,0:T(8,128)S(1)} %bitcast.1, f32[256]{0:T(256)S(1)} %copy-done.2, s32[1,32]{1,0:T(1,128)S(1)} %copy-done.3, f32[512,256]{1,0:T(8,128)S(1)} %and_select_fusion.pool_ref), custom_call_target="tpu_custom_call" | custom-call | tf_op jit(solution)/shard_map/pallas_call | solution.py:360
  77.8 1.0 %copy.8 = f32[64,32,128]{2,1,0:T(8,128)} copy(f32[64,32,128]{2,1,0:T(8,128)S(1)} %get-tuple-element.8) | data formatting | bytes 2097152
  78.8 0.7 copy.9
  (2 shorter events, 0.0 us)
Async XLA Ops:
  0.7 0.7 copy-start.1
  0.7 0.7 copy-start.2
  0.7 0.7 copy-start.3
  1.4 1.2 %copy-start = (f32[64,32,128]{2,1,0:T(8,128)S(1)}, f32[64,32,128]{2,1,0:T(8,128)}, u32[]{:S(2)}) copy-start(f32[64,32,128]{2,1,0:T(8,128)} %rhs_ref.1) | copy-start | bytes 3145732

commit v2 on v1

--- a/solution.py
+++ b/solution.py
@@ -9,7 +9,7 @@
 
 SWEEPS = 2
 SOLVES = 2 * SWEEPS
-UNROLL = 4
+UNROLL = 8
 MESH = pl.DeviceIdType.MESH
 
 
@@ -122,22 +122,25 @@
         up_spike[k] = high
         return g, low, high
 
-    def around(cells, left_edge, right_edge):
-        left = jnp.where(at_left, left_edge, pltpu.roll(cells, 1, 1))
-        right = jnp.where(at_right, right_edge, pltpu.roll(cells, width - 1, 1))
+    def turned(cells, shift):
+        shift = shift % width
+        return cells if shift == 0 else pltpu.roll(cells, shift, 1)
+
+    def around(cells, edge, edge_mask):
+        left = jnp.where(at_left, 0.0, pltpu.roll(cells, 1, 1))
+        right = jnp.where(at_right, 0.0, pltpu.roll(cells, width - 1, 1))
         up = jnp.where(at_top, 0.0, pltpu.roll(cells, 1, 0))
         down = jnp.where(at_bottom, 0.0, pltpu.roll(cells, rows - 1, 0))
-        return (left + right) + (up + down)
-
-    def next_edge(edge):
-        return pltpu.roll(edge, width - 1, 1)
-
-    def forward(k, carry):
-        d_before, left_edge, right_edge = carry
-        side = rhs_ref[k] + around(p_ref[k], left_edge, right_edge)
-        d = side * side_inv[k] - low_inv[k] * d_before
-        local[k] = d
-        return d, next_edge(left_edge), next_edge(right_edge)
+        return (left + right) + (up + down) + jnp.where(edge_mask, edge, 0.0)
+
+    def forward(edge_mask, step, carry):
+        d, edges = carry
+        for j in range(UNROLL):
+            k = step * UNROLL + j
+            side = rhs_ref[k] + around(p_ref[k], turned(edges, -j), edge_mask)
+            d = side * side_inv[k] - low_inv[k] * d
+            local[k] = d
+        return d, turned(edges, -UNROLL)
 
     def backward(i, g_after):
         k = levels - 1 - i
@@ -175,7 +178,7 @@
         def _():
             to_left.start()
 
-    def finish_halo(t):
+    def finish_halo(t, colour):
         to_right, to_left = halo_copies(t)
 
         @pl.when(gx > 0)
@@ -190,7 +193,8 @@
 
         left_edge = pltpu.roll(halo_in[t, 0], levels % width, 1)
         right_edge = pltpu.roll(halo_in[t, 1], (levels - 2) % width, 1)
-        return left_edge, right_edge
+        needs_left = lax.rem(row + gx * width, 2) == colour
+        return jnp.where(needs_left, left_edge, right_edge)
 
     def column_copy(ref, send, recv, o):
         return pltpu.make_async_remote_copy(
@@ -213,9 +217,12 @@
             spikes[gz, 2] = high
             spikes[gz, 3] = up_spike[levels - 1]
         else:
-            left_edge, right_edge = finish_halo(t - 1)
-            d_last, _, _ = lax.fori_loop(
-                0, levels, forward, (zero, left_edge, right_edge), unroll=UNROLL
+            edge_mask = (at_left | at_right) & (parity == colour)
+            d_last, _ = lax.fori_loop(
+                0,
+                levels // UNROLL,
+                functools.partial(forward, edge_mask),
+                (zero, finish_halo(t - 1, colour)),
             )
             g = lax.fori_loop(0, levels, backward, zero, unroll=UNROLL)
         ends[t, gz, 0] = g
@@ -257,35 +264,38 @@
         below_value = lasts[gz]
         above_value = firsts[gz + 1]
 
-        def correct(k, carry):
-            to_right, to_left = carry
-            value = local[k] + low_spike[k] * below_value + up_spike[k] * above_value
-            before = zero if t == 0 else p_ref[k]
-            cells = jnp.where(parity == colour, value, before)
-            p_ref[k] = cells
-            if t == SOLVES - 1:
-                cells = cells - before
-                delta[k] = cells
-            to_right = jnp.where(at_right, cells, next_edge(to_right))
-            to_left = jnp.where(at_left, cells, next_edge(to_left))
+        def correct(step, carry):
+            to_right, to_left = (turned(edge, -UNROLL) for edge in carry)
+            for j in range(UNROLL):
+                k = step * UNROLL + j
+                value = local[k] + low_spike[k] * below_value + up_spike[k] * above_value
+                before = zero if t == 0 else p_ref[k]
+                cells = jnp.where(parity == colour, value, before)
+                p_ref[k] = cells
+                if t == SOLVES - 1:
+                    cells = cells - before
+                    delta[k] = cells
+                moved = turned(cells, 1 + j - UNROLL)
+                to_right = jnp.where(lane == width - UNROLL + j, moved, to_right)
+                to_left = jnp.where(lane == (width + 1 - UNROLL + j) % width, moved, to_left)
             return to_right, to_left
 
-        to_right, to_left = lax.fori_loop(0, levels, correct, (zero, zero), unroll=UNROLL)
+        to_right, to_left = lax.fori_loop(0, levels // UNROLL, correct, (zero, zero))
         halo_out[t, 0] = to_right
         halo_out[t, 1] = to_left
         start_halo(t)
 
-    def coarsen(i, carry):
-        left_edge, right_edge = carry
-        total = zero
-        for j in range(2):
-            k = 2 * i + j
-            total += fluid_at(k) * around(delta[k], left_edge, right_edge)
-            left_edge, right_edge = next_edge(left_edge), next_edge(right_edge)
-        local[i] = total
-        return left_edge, right_edge
-
-    lax.fori_loop(0, levels // 2, coarsen, finish_halo(SOLVES - 1), unroll=2)
+    edge_mask = (at_left | at_right) & (parity == 0)
+
+    def coarsen(step, edges):
+        for j in range(0, UNROLL, 2):
+            k = step * UNROLL + j
+            local[step * (UNROLL // 2) + j // 2] = fluid_at(k) * around(
+                delta[k], turned(edges, -j), edge_mask
+            ) + fluid_at(k + 1) * around(delta[k + 1], turned(edges, -j - 1), edge_mask)
+        return turned(edges, -UNROLL)
+
+    lax.fori_loop(0, levels // UNROLL, coarsen, finish_halo(SOLVES - 1, 0))
 
     half = rows // 2
     per_row = width // (width // 4)

time: 79.7 us -> 53 us (0.66)
  Pallas kernels: 75.2 us -> 48.5 us
    pallas_call x1, Pallas kernels: 75.2 us -> 48.5 us  [on_device(): pl.pallas_call(functools.partial(relax_kernel, n_gz, n_gx), out_shape=(ja...]
where the time goes in v2:
time: 53 us; the launch traced here: 52.7 us
  Pallas kernels  48.5 us (92%)
  local copies, waits for them, and re-layouts  3.34 us (6%)
  between operations  0.68 us (1%)
    pallas_call x1, Pallas kernels, on_device(): pl.pallas_call(functools.partial(relax_kernel, n_gz, n_gx), out_shape=(ja...  48.5 us
    unnamed x10, local copies, waits for them, and re-layouts  3.34 us

profile of v2, /device:TPU:0, one launch (start us, length us, event | category | flops | bytes accessed | tf_op | source)
XLA Modules:
  0.0 52.7 jit_solution(8524321390456600978)
XLA Ops:
  0.7 0.0 copy-start.1
  0.7 0.0 copy-start.2
  0.7 0.0 copy-start.3
  0.7 0.2 and_select_fusion.pool_ref
  0.9 0.5 copy-done.1
  1.4 0.0 copy-done.2
  1.4 0.0 copy-done.3
  1.4 0.0 copy-start
  1.4 1.2 %copy-done = f32[64,32,128]{2,1,0:T(8,128)S(1)} copy-done((f32[64,32,128]{2,1,0:T(8,128)S(1)}, f32[64,32,128]{2,1,0:T(8,128)}, u32[]{:S(2)}) %copy-start) | copy-done | bytes 1048600
  2.6 48.5 %shard_map.59 = (f32[64,32,128]{2,1,0:T(8,128)S(1)}, f32[32,1024]{1,0:T(8,128)S(1)}) custom-call(f32[64,32,128]{2,1,0:T(8,128)S(1)} %copy-done, s32[32,128]{1,0:T(8,128)S(1)} %bitcast.1, f32[256]{0:T(256)S(1)} %copy-done.2, s32[1,32]{1,0:T(1,128)S(1)} %copy-done.3, f32[512,256]{1,0:T(8,128)S(1)} %and_select_fusion.pool_ref), custom_call_target="tpu_custom_call" | custom-call | tf_op jit(solution)/shard_map/pallas_call | solution.py:370
  51.1 1.0 %copy.8 = f32[64,32,128]{2,1,0:T(8,128)} copy(f32[64,32,128]{2,1,0:T(8,128)S(1)} %get-tuple-element.8) | data formatting | bytes 2097152
  52.1 0.7 %copy.9 = f32[32,1024]{1,0:T(8,128)} copy(f32[32,1024]{1,0:T(8,128)S(1)} %get-tuple-element.9) | data formatting | bytes 262144
  (2 shorter events, 0.0 us)
Async XLA Ops:
  0.7 0.7 %copy-start.1 = (s32[128,32]{0,1:T(8,128)S(1)}, s32[128,32]{0,1:T(8,128)}, u32[]{:S(2)}) copy-start(s32[128,32]{0,1:T(8,128)} %param.5) | copy-start | bytes 49156
  0.7 0.7 %copy-start.2 = (f32[256]{0:T(256)S(1)}, f32[256]{0:T(256)}, u32[]{:S(2)}) copy-start(f32[256]{0:T(256)} %coef_ref.1) | copy-start | bytes 3076
  0.7 0.7 %copy-start.3 = (s32[1,32]{1,0:T(1,128)S(1)}, s32[1,32]{1,0:T(1,128)}, u32[]{:S(2)}) copy-start(s32[1,32]{1,0:T(1,128)} %balance_ref.1) | copy-start | bytes 388
  1.4 1.2 %copy-start = (f32[64,32,128]{2,1,0:T(8,128)S(1)}, f32[64,32,128]{2,1,0:T(8,128)}, u32[]{:S(2)}) copy-start(f32[64,32,128]{2,1,0:T(8,128)} %rhs_ref.1) | copy-start | bytes 3145732

commit v3 on v2

--- a/solution.py
+++ b/solution.py
@@ -35,6 +35,7 @@
     reduced,
     firsts,
     lasts,
+    edge_spikes,
     halo_out,
     halo_in,
     pooled,
@@ -110,18 +111,6 @@
         low_spike[k] = spike
         return up, d, spike
 
-    def factor_back(i, carry):
-        k = levels - 1 - i
-        g_after, low_after, up_after = carry
-        up = upper[k]
-        g = local[k] - up * g_after
-        low = low_spike[k] - up * low_after
-        high = -up * up_after
-        local[k] = g
-        low_spike[k] = low
-        up_spike[k] = high
-        return g, low, high
-
     def turned(cells, shift):
         shift = shift % width
         return cells if shift == 0 else pltpu.roll(cells, shift, 1)
@@ -142,15 +131,52 @@
             local[k] = d
         return d, turned(edges, -UNROLL)
 
-    def backward(i, g_after):
-        k = levels - 1 - i
-        g = local[k] - upper[k] * g_after
-        local[k] = g
-        return g
+    def with_edge(packed, cells, i, offset):
+        return jnp.where(lane == i + offset, turned(cells, i + 1), packed)
+
+    def factor_back(step, carry):
+        g, low, high, g_edge, low_right, low_left, high_right, high_left = carry
+        base = levels - UNROLL * (step + 1)
+        g_edge, low_right, low_left, high_right, high_left = (
+            turned(edge, UNROLL)
+            for edge in (g_edge, low_right, low_left, high_right, high_left)
+        )
+        for i in reversed(range(UNROLL)):
+            k = base + i
+            up = upper[k]
+            g = local[k] - up * g
+            low = low_spike[k] - up * low
+            high = -up * high
+            local[k] = g
+            low_spike[k] = low
+            up_spike[k] = high
+            g_edge = with_edge(g_edge, g, i, edge_lane(0))
+            low_right = with_edge(low_right, low, i, 0)
+            low_left = with_edge(low_left, low, i, 1)
+            high_right = with_edge(high_right, high, i, 0)
+            high_left = with_edge(high_left, high, i, 1)
+        return g, low, high, g_edge, low_right, low_left, high_right, high_left
+
+    def backward(offset, step, carry):
+        g, g_edge = carry
+        base = levels - UNROLL * (step + 1)
+        g_edge = turned(g_edge, UNROLL)
+        for i in reversed(range(UNROLL)):
+            k = base + i
+            g = local[k] - upper[k] * g
+            local[k] = g
+            g_edge = with_edge(g_edge, g, i, offset)
+        return g, g_edge
+
+    def from_left(colour):
+        return lax.rem(row + gx * width, 2) == colour
+
+    def edge_lane(colour):
+        return jnp.where(from_left(colour), 1, 0)
 
     def halo_copies(t):
         to_right = pltpu.make_async_remote_copy(
-            src_ref=halo_out.at[t, 0],
+            src_ref=halo_out.at[t],
             dst_ref=halo_in.at[t, 0],
             send_sem=halo_send.at[t, 0],
             recv_sem=halo_recv.at[t, 0],
@@ -158,7 +184,7 @@
             device_id_type=MESH,
         )
         to_left = pltpu.make_async_remote_copy(
-            src_ref=halo_out.at[t, 1],
+            src_ref=halo_out.at[t],
             dst_ref=halo_in.at[t, 1],
             send_sem=halo_send.at[t, 1],
             recv_sem=halo_recv.at[t, 1],
@@ -191,15 +217,14 @@
             to_right.wait_send()
             to_left.wait_recv()
 
-        left_edge = pltpu.roll(halo_in[t, 0], levels % width, 1)
-        right_edge = pltpu.roll(halo_in[t, 1], (levels - 2) % width, 1)
-        needs_left = lax.rem(row + gx * width, 2) == colour
-        return jnp.where(needs_left, left_edge, right_edge)
+        left_edge = halo_in[t, 0]
+        right_edge = turned(halo_in[t, 1], -2)
+        return jnp.where(from_left(colour), left_edge, right_edge)
 
     def column_copy(ref, send, recv, o):
         return pltpu.make_async_remote_copy(
-            src_ref=ref.at[gz],
-            dst_ref=ref.at[gz],
+            src_ref=ref,
+            dst_ref=ref,
             send_sem=send.at[o - 1],
             recv_sem=recv.at[o - 1],
             device_id=(gx, lax.rem(gz + o, n_gz)),
@@ -211,11 +236,24 @@
         if t == 0:
             lax.fori_loop(0, levels, factor, (zero, zero, one), unroll=UNROLL)
             d_last = local[levels - 1]
-            g, low, high = lax.fori_loop(0, levels, factor_back, (zero, zero, one), unroll=UNROLL)
-            spikes[gz, 0] = low
-            spikes[gz, 1] = low_spike[levels - 1]
-            spikes[gz, 2] = high
-            spikes[gz, 3] = up_spike[levels - 1]
+            spikes[gz, 0] = low_spike[levels - 1]
+            spikes[gz, 1] = -upper[levels - 1]
+            pl.semaphore_wait(barrier, n_gz + n_gx - 2)
+            early = [
+                column_copy(
+                    spikes.at[gz, pl.ds(0, 2)], spikes_send.at[0], spikes_recv.at[0], o
+                )
+                for o in range(1, n_gz)
+            ]
+            for copy in early:
+                copy.start()
+            g, low, high, g_edge, *spike_edges = lax.fori_loop(
+                0, levels // UNROLL, factor_back, (zero, zero, one) + (zero,) * 5
+            )
+            spikes[gz, 2] = low
+            spikes[gz, 3] = high
+            for e in range(4):
+                edge_spikes[e] = spike_edges[e]
         else:
             edge_mask = (at_left | at_right) & (parity == colour)
             d_last, _ = lax.fori_loop(
@@ -224,34 +262,46 @@
                 functools.partial(forward, edge_mask),
                 (zero, finish_halo(t - 1, colour)),
             )
-            g = lax.fori_loop(0, levels, backward, zero, unroll=UNROLL)
+            g, g_edge = lax.fori_loop(
+                0,
+                levels // UNROLL,
+                functools.partial(backward, edge_lane(colour)),
+                (zero, zero),
+            )
         ends[t, gz, 0] = g
         ends[t, gz, 1] = d_last
         copies = [
-            column_copy(ends.at[t], ends_send.at[t], ends_recv.at[t], o) for o in range(1, n_gz)
+            column_copy(ends.at[t, gz], ends_send.at[t], ends_recv.at[t], o)
+            for o in range(1, n_gz)
         ]
         if t == 0:
-            copies += [column_copy(spikes, spikes_send, spikes_recv, o) for o in range(1, n_gz)]
-            pl.semaphore_wait(barrier, n_gz + n_gx - 2)
+            copies += [
+                column_copy(
+                    spikes.at[gz, pl.ds(2, 2)], spikes_send.at[1], spikes_recv.at[1], o
+                )
+                for o in range(1, n_gz)
+            ]
         for copy in copies:
             copy.start()
+        if t == 0:
+            copies += early
         for copy in copies:
             copy.wait()
 
         if t == 0:
             beta = zero
             for s in range(n_gz):
-                inverse = 1.0 / (1.0 - spikes[s, 0] * beta)
+                inverse = 1.0 / (1.0 - spikes[s, 2] * beta)
                 reduced[s, 0] = beta
                 reduced[s, 1] = inverse
-                reduced[s, 2] = spikes[s, 2] * inverse
-                beta = spikes[s, 3] + spikes[s, 1] * beta * reduced[s, 2]
+                reduced[s, 2] = spikes[s, 3] * inverse
+                beta = spikes[s, 1] + spikes[s, 0] * beta * reduced[s, 2]
                 reduced[s, 3] = beta
         alpha = zero
         heads, tails = [], []
         for s in range(n_gz):
-            head = (ends[t, s, 0] + spikes[s, 0] * alpha) * reduced[s, 1]
-            alpha = ends[t, s, 1] + spikes[s, 1] * (alpha + reduced[s, 0] * head)
+            head = (ends[t, s, 0] + spikes[s, 2] * alpha) * reduced[s, 1]
+            alpha = ends[t, s, 1] + spikes[s, 0] * (alpha + reduced[s, 0] * head)
             heads.append(head)
             tails.append(alpha)
         after = zero
@@ -264,26 +314,27 @@
         below_value = lasts[gz]
         above_value = firsts[gz + 1]
 
-        def correct(step, carry):
-            to_right, to_left = (turned(edge, -UNROLL) for edge in carry)
-            for j in range(UNROLL):
-                k = step * UNROLL + j
-                value = local[k] + low_spike[k] * below_value + up_spike[k] * above_value
-                before = zero if t == 0 else p_ref[k]
-                cells = jnp.where(parity == colour, value, before)
-                p_ref[k] = cells
-                if t == SOLVES - 1:
-                    cells = cells - before
-                    delta[k] = cells
-                moved = turned(cells, 1 + j - UNROLL)
-                to_right = jnp.where(lane == width - UNROLL + j, moved, to_right)
-                to_left = jnp.where(lane == (width + 1 - UNROLL + j) % width, moved, to_left)
-            return to_right, to_left
-
-        to_right, to_left = lax.fori_loop(0, levels // UNROLL, correct, (zero, zero))
-        halo_out[t, 0] = to_right
-        halo_out[t, 1] = to_left
+        sent = from_left(colour)
+        below_edge = jnp.where(sent, below_value[:, :1], below_value[:, width - 1 :])
+        above_edge = jnp.where(sent, above_value[:, :1], above_value[:, width - 1 :])
+        low_edge = jnp.where(sent, edge_spikes[1], edge_spikes[0])
+        high_edge = jnp.where(sent, edge_spikes[3], edge_spikes[2])
+        edge_cells = g_edge + low_edge * below_edge + high_edge * above_edge
+        if t == SOLVES - 1:
+            edge_cells = edge_cells - halo_out[t - 2]
+        halo_out[t] = edge_cells
         start_halo(t)
+
+        def correct(k, carry):
+            value = local[k] + low_spike[k] * below_value + up_spike[k] * above_value
+            before = zero if t == 0 else p_ref[k]
+            cells = jnp.where(parity == colour, value, before)
+            p_ref[k] = cells
+            if t == SOLVES - 1:
+                delta[k] = cells - before
+            return carry
+
+        lax.fori_loop(0, levels, correct, 0, unroll=UNROLL)
 
     edge_mask = (at_left | at_right) & (parity == 0)
 
@@ -382,7 +433,8 @@
             planes(n_gz, 4),
             planes(n_gz + 1),
             planes(n_gz + 1),
-            planes(SOLVES, 2),
+            planes(4),
+            planes(SOLVES),
             planes(SOLVES, 2),
             pltpu.VMEM((chunks * rows // 2, per_row * width), jnp.float32),
             pltpu.VMEM((rows, chunks, width), jnp.float32),
@@ -390,8 +442,8 @@
             pltpu.VMEM((rows, chunks, width), jnp.float32),
             sems(SOLVES, n_gz - 1),
             sems(SOLVES, n_gz - 1),
-            sems(n_gz - 1),
-            sems(n_gz - 1),
+            sems(2, n_gz - 1),
+            sems(2, n_gz - 1),
             sems(SOLVES, 2),
             sems(SOLVES, 2),
             sems(n_gx - 1),

time: 53 us -> 51.7 us (0.975)
  Pallas kernels: 48.5 us -> 47.2 us
    pallas_call x1, Pallas kernels: 48.5 us -> 47.2 us  [on_device(): pl.pallas_call(functools.partial(relax_kernel, n_gz, n_gx), out_shape=(ja...]
where the time goes in v3:
time: 51.7 us; the launch traced here: 51.4 us
  Pallas kernels  47.2 us (91%)
  local copies, waits for them, and re-layouts  3.34 us (6%)
  between operations  0.68 us (1%)
    pallas_call x1, Pallas kernels, on_device(): pl.pallas_call(functools.partial(relax_kernel, n_gz, n_gx), out_shape=(ja...  47.2 us
    unnamed x10, local copies, waits for them, and re-layouts  3.34 us

profile of v3, /device:TPU:0, one launch (start us, length us, event | category | flops | bytes accessed | tf_op | source)
XLA Modules:
  0.0 51.4 jit_solution(8146834527146921663)
XLA Ops:
  0.7 0.0 copy-start.1
  0.7 0.0 copy-start.2
  0.7 0.0 copy-start.3
  0.7 0.2 and_select_fusion.pool_ref
  0.9 0.5 copy-done.1
  1.4 0.0 copy-done.2
  1.4 0.0 copy-done.3
  1.4 0.0 copy-start
  1.4 1.2 %copy-done = f32[64,32,128]{2,1,0:T(8,128)S(1)} copy-done((f32[64,32,128]{2,1,0:T(8,128)S(1)}, f32[64,32,128]{2,1,0:T(8,128)}, u32[]{:S(2)}) %copy-start) | copy-done | bytes 1048600
  2.6 47.2 %shard_map.59 = (f32[64,32,128]{2,1,0:T(8,128)S(1)}, f32[32,1024]{1,0:T(8,128)S(1)}) custom-call(f32[64,32,128]{2,1,0:T(8,128)S(1)} %copy-done, s32[32,128]{1,0:T(8,128)S(1)} %bitcast.1, f32[256]{0:T(256)S(1)} %copy-done.2, s32[1,32]{1,0:T(1,128)S(1)} %copy-done.3, f32[512,256]{1,0:T(8,128)S(1)} %and_select_fusion.pool_ref), custom_call_target="tpu_custom_call" | custom-call | tf_op jit(solution)/shard_map/pallas_call | solution.py:421
  49.8 1.0 %copy.8 = f32[64,32,128]{2,1,0:T(8,128)} copy(f32[64,32,128]{2,1,0:T(8,128)S(1)} %get-tuple-element.8) | data formatting | bytes 2097152
  50.8 0.7 %copy.9 = f32[32,1024]{1,0:T(8,128)} copy(f32[32,1024]{1,0:T(8,128)S(1)} %get-tuple-element.9) | data formatting | bytes 262144
  (2 shorter events, 0.0 us)
Async XLA Ops:
  0.7 0.7 %copy-start.1 = (s32[128,32]{0,1:T(8,128)S(1)}, s32[128,32]{0,1:T(8,128)}, u32[]{:S(2)}) copy-start(s32[128,32]{0,1:T(8,128)} %param.5) | copy-start | bytes 49156
  0.7 0.7 %copy-start.2 = (f32[256]{0:T(256)S(1)}, f32[256]{0:T(256)}, u32[]{:S(2)}) copy-start(f32[256]{0:T(256)} %coef_ref.1) | copy-start | bytes 3076
  0.7 0.7 %copy-start.3 = (s32[1,32]{1,0:T(1,128)S(1)}, s32[1,32]{1,0:T(1,128)}, u32[]{:S(2)}) copy-start(s32[1,32]{1,0:T(1,128)} %balance_ref.1) | copy-start | bytes 388
  1.4 1.2 %copy-start = (f32[64,32,128]{2,1,0:T(8,128)S(1)}, f32[64,32,128]{2,1,0:T(8,128)}, u32[]{:S(2)}) copy-start(f32[64,32,128]{2,1,0:T(8,128)} %rhs_ref.1) | copy-start | bytes 3145732

commit v4 on v3

--- a/solution.py
+++ b/solution.py
@@ -238,15 +238,6 @@
             d_last = local[levels - 1]
             spikes[gz, 0] = low_spike[levels - 1]
             spikes[gz, 1] = -upper[levels - 1]
-            pl.semaphore_wait(barrier, n_gz + n_gx - 2)
-            early = [
-                column_copy(
-                    spikes.at[gz, pl.ds(0, 2)], spikes_send.at[0], spikes_recv.at[0], o
-                )
-                for o in range(1, n_gz)
-            ]
-            for copy in early:
-                copy.start()
             g, low, high, g_edge, *spike_edges = lax.fori_loop(
                 0, levels // UNROLL, factor_back, (zero, zero, one) + (zero,) * 5
             )
@@ -268,23 +259,18 @@
                 functools.partial(backward, edge_lane(colour)),
                 (zero, zero),
             )
-        ends[t, gz, 0] = g
-        ends[t, gz, 1] = d_last
+        ends[t, gz] = jnp.where(parity == colour, g, turned(d_last, 1))
         copies = [
             column_copy(ends.at[t, gz], ends_send.at[t], ends_recv.at[t], o)
             for o in range(1, n_gz)
         ]
         if t == 0:
             copies += [
-                column_copy(
-                    spikes.at[gz, pl.ds(2, 2)], spikes_send.at[1], spikes_recv.at[1], o
-                )
-                for o in range(1, n_gz)
+                column_copy(spikes.at[gz], spikes_send, spikes_recv, o) for o in range(1, n_gz)
             ]
+            pl.semaphore_wait(barrier, n_gz + n_gx - 2)
         for copy in copies:
             copy.start()
-        if t == 0:
-            copies += early
         for copy in copies:
             copy.wait()
 
@@ -300,8 +286,9 @@
         alpha = zero
         heads, tails = [], []
         for s in range(n_gz):
-            head = (ends[t, s, 0] + spikes[s, 2] * alpha) * reduced[s, 1]
-            alpha = ends[t, s, 1] + spikes[s, 0] * (alpha + reduced[s, 0] * head)
+            both = ends[t, s]
+            head = (both + spikes[s, 2] * alpha) * reduced[s, 1]
+            alpha = turned(both, -1) + spikes[s, 0] * (alpha + reduced[s, 0] * head)
             heads.append(head)
             tails.append(alpha)
         after = zero
@@ -428,7 +415,7 @@
         out_specs=(vmem, vmem),
         scratch_shapes=[slab] * 7
         + [
-            planes(SOLVES, n_gz, 2),
+            planes(SOLVES, n_gz),
             planes(n_gz, 4),
             planes(n_gz, 4),
             planes(n_gz + 1),
@@ -442,8 +429,8 @@
             pltpu.VMEM((rows, chunks, width), jnp.float32),
             sems(SOLVES, n_gz - 1),
             sems(SOLVES, n_gz - 1),
-            sems(2, n_gz - 1),
-            sems(2, n_gz - 1),
+            sems(n_gz - 1),
+            sems(n_gz - 1),
             sems(SOLVES, 2),
             sems(SOLVES, 2),
             sems(n_gx - 1),

time: 51.7 us -> 51 us (0.986)
  Pallas kernels: 47.2 us -> 46.5 us
    pallas_call x1, Pallas kernels: 47.2 us -> 46.5 us  [on_device(): pl.pallas_call(functools.partial(relax_kernel, n_gz, n_gx), out_shape=(ja...]
where the time goes in v4:
time: 51 us; the launch traced here: 50.7 us
  Pallas kernels  46.5 us (91%)
  local copies, waits for them, and re-layouts  3.34 us (7%)
  between operations  0.68 us (1%)
    pallas_call x1, Pallas kernels, on_device(): pl.pallas_call(functools.partial(relax_kernel, n_gz, n_gx), out_shape=(ja...  46.5 us
    unnamed x10, local copies, waits for them, and re-layouts  3.34 us

profile of v4, /device:TPU:0, one launch (start us, length us, event | category | flops | bytes accessed | tf_op | source)
XLA Modules:
  0.0 50.7 jit_solution(11555698865873399164)
XLA Ops:
  0.7 0.0 copy-start.1
  0.7 0.0 copy-start.2
  0.7 0.0 copy-start.3
  0.7 0.2 and_select_fusion.pool_ref
  0.9 0.5 copy-done.1
  1.4 0.0 copy-done.2
  1.4 0.0 copy-done.3
  1.4 0.0 copy-start
  1.4 1.2 %copy-done = f32[64,32,128]{2,1,0:T(8,128)S(1)} copy-done((f32[64,32,128]{2,1,0:T(8,128)S(1)}, f32[64,32,128]{2,1,0:T(8,128)}, u32[]{:S(2)}) %copy-start) | copy-done | bytes 1048600
  2.6 46.5 %shard_map.59 = (f32[64,32,128]{2,1,0:T(8,128)S(1)}, f32[32,1024]{1,0:T(8,128)S(1)}) custom-call(f32[64,32,128]{2,1,0:T(8,128)S(1)} %copy-done, s32[32,128]{1,0:T(8,128)S(1)} %bitcast.1, f32[256]{0:T(256)S(1)} %copy-done.2, s32[1,32]{1,0:T(1,128)S(1)} %copy-done.3, f32[512,256]{1,0:T(8,128)S(1)} %and_select_fusion.pool_ref), custom_call_target="tpu_custom_call" | custom-call | tf_op jit(solution)/shard_map/pallas_call | solution.py:408
  49.1 1.0 %copy.8 = f32[64,32,128]{2,1,0:T(8,128)} copy(f32[64,32,128]{2,1,0:T(8,128)S(1)} %get-tuple-element.8) | data formatting | bytes 2097152
  50.1 0.7 %copy.9 = f32[32,1024]{1,0:T(8,128)} copy(f32[32,1024]{1,0:T(8,128)S(1)} %get-tuple-element.9) | data formatting | bytes 262144
  (2 shorter events, 0.0 us)
Async XLA Ops:
  0.7 0.7 %copy-start.1 = (s32[128,32]{0,1:T(8,128)S(1)}, s32[128,32]{0,1:T(8,128)}, u32[]{:S(2)}) copy-start(s32[128,32]{0,1:T(8,128)} %param.5) | copy-start | bytes 49156
  0.7 0.7 %copy-start.2 = (f32[256]{0:T(256)S(1)}, f32[256]{0:T(256)}, u32[]{:S(2)}) copy-start(f32[256]{0:T(256)} %coef_ref.1) | copy-start | bytes 3076
  0.7 0.7 %copy-start.3 = (s32[1,32]{1,0:T(1,128)S(1)}, s32[1,32]{1,0:T(1,128)}, u32[]{:S(2)}) copy-start(s32[1,32]{1,0:T(1,128)} %balance_ref.1) | copy-start | bytes 388
  1.4 1.2 %copy-start = (f32[64,32,128]{2,1,0:T(8,128)S(1)}, f32[64,32,128]{2,1,0:T(8,128)}, u32[]{:S(2)}) copy-start(f32[64,32,128]{2,1,0:T(8,128)} %rhs_ref.1) | copy-start | bytes 3145732

commit v5 on v3

--- a/solution.py
+++ b/solution.py
@@ -268,8 +268,7 @@
                 functools.partial(backward, edge_lane(colour)),
                 (zero, zero),
             )
-        ends[t, gz, 0] = g
-        ends[t, gz, 1] = d_last
+        ends[t, gz] = jnp.where(parity == colour, g, turned(d_last, 1))
         copies = [
             column_copy(ends.at[t, gz], ends_send.at[t], ends_recv.at[t], o)
             for o in range(1, n_gz)
@@ -300,8 +299,9 @@
         alpha = zero
         heads, tails = [], []
         for s in range(n_gz):
-            head = (ends[t, s, 0] + spikes[s, 2] * alpha) * reduced[s, 1]
-            alpha = ends[t, s, 1] + spikes[s, 0] * (alpha + reduced[s, 0] * head)
+            both = ends[t, s]
+            head = (both + spikes[s, 2] * alpha) * reduced[s, 1]
+            alpha = turned(both, -1) + spikes[s, 0] * (alpha + reduced[s, 0] * head)
             heads.append(head)
             tails.append(alpha)
         after = zero
@@ -428,7 +428,7 @@
         out_specs=(vmem, vmem),
         scratch_shapes=[slab] * 7
         + [
-            planes(SOLVES, n_gz, 2),
+            planes(SOLVES, n_gz),
             planes(n_gz, 4),
             planes(n_gz, 4),
             planes(n_gz + 1),

time: 51.7 us -> 50.8 us (0.983)
  Pallas kernels: 47.2 us -> 46.3 us
    pallas_call x1, Pallas kernels: 47.2 us -> 46.3 us  [on_device(): pl.pallas_call(functools.partial(relax_kernel, n_gz, n_gx), out_shape=(ja...]
where the time goes in v5:
time: 50.8 us; the launch traced here: 50.5 us
  Pallas kernels  46.3 us (91%)
  local copies, waits for them, and re-layouts  3.34 us (7%)
  between operations  0.68 us (1%)
    pallas_call x1, Pallas kernels, on_device(): pl.pallas_call(functools.partial(relax_kernel, n_gz, n_gx), out_shape=(ja...  46.3 us
    unnamed x10, local copies, waits for them, and re-layouts  3.34 us

profile of v5, /device:TPU:0, one launch (start us, length us, event | category | flops | bytes accessed | tf_op | source)
XLA Modules:
  0.0 50.5 jit_solution(2547089089866919881)
XLA Ops:
  0.7 0.0 copy-start.1
  0.7 0.0 copy-start.2
  0.7 0.0 copy-start.3
  0.7 0.2 and_select_fusion.pool_ref
  0.9 0.5 copy-done.1
  1.4 0.0 copy-done.2
  1.4 0.0 copy-done.3
  1.4 0.0 copy-start
  1.4 1.2 %copy-done = f32[64,32,128]{2,1,0:T(8,128)S(1)} copy-done((f32[64,32,128]{2,1,0:T(8,128)S(1)}, f32[64,32,128]{2,1,0:T(8,128)}, u32[]{:S(2)}) %copy-start) | copy-done | bytes 1048600
  2.6 46.3 %shard_map.59 = (f32[64,32,128]{2,1,0:T(8,128)S(1)}, f32[32,1024]{1,0:T(8,128)S(1)}) custom-call(f32[64,32,128]{2,1,0:T(8,128)S(1)} %copy-done, s32[32,128]{1,0:T(8,128)S(1)} %bitcast.1, f32[256]{0:T(256)S(1)} %copy-done.2, s32[1,32]{1,0:T(1,128)S(1)} %copy-done.3, f32[512,256]{1,0:T(8,128)S(1)} %and_select_fusion.pool_ref), custom_call_target="tpu_custom_call" | custom-call | tf_op jit(solution)/shard_map/pallas_call | solution.py:421
  48.9 1.0 %copy.8 = f32[64,32,128]{2,1,0:T(8,128)} copy(f32[64,32,128]{2,1,0:T(8,128)S(1)} %get-tuple-element.8) | data formatting | bytes 2097152
  49.9 0.7 %copy.9 = f32[32,1024]{1,0:T(8,128)} copy(f32[32,1024]{1,0:T(8,128)S(1)} %get-tuple-element.9) | data formatting | bytes 262144
  (2 shorter events, 0.0 us)
Async XLA Ops:
  0.7 0.7 %copy-start.1 = (s32[128,32]{0,1:T(8,128)S(1)}, s32[128,32]{0,1:T(8,128)}, u32[]{:S(2)}) copy-start(s32[128,32]{0,1:T(8,128)} %param.5) | copy-start | bytes 49156
  0.7 0.7 %copy-start.2 = (f32[256]{0:T(256)S(1)}, f32[256]{0:T(256)}, u32[]{:S(2)}) copy-start(f32[256]{0:T(256)} %coef_ref.1) | copy-start | bytes 3076
  0.7 0.7 %copy-start.3 = (s32[1,32]{1,0:T(1,128)S(1)}, s32[1,32]{1,0:T(1,128)}, u32[]{:S(2)}) copy-start(s32[1,32]{1,0:T(1,128)} %balance_ref.1) | copy-start | bytes 388
  1.4 1.2 %copy-start = (f32[64,32,128]{2,1,0:T(8,128)S(1)}, f32[64,32,128]{2,1,0:T(8,128)}, u32[]{:S(2)}) copy-start(f32[64,32,128]{2,1,0:T(8,128)} %rhs_ref.1) | copy-start | bytes 3145732

commit v6 on v5

--- a/solution.py
+++ b/solution.py
@@ -285,7 +285,7 @@
         if t == 0:
             copies += early
         for copy in copies:
-            copy.wait()
+            copy.wait_recv()
 
         if t == 0:
             beta = zero
@@ -335,6 +335,8 @@
             return carry
 
         lax.fori_loop(0, levels, correct, 0, unroll=UNROLL)
+        for copy in copies:
+            copy.wait_send()
 
     edge_mask = (at_left | at_right) & (parity == 0)
 

time: 50.8 us -> 50.8 us (level)
  no operation moved by 1% of the time
where the time goes in v6:
time: 50.8 us; the launch traced here: 50.5 us
  Pallas kernels  46.3 us (91%)
  local copies, waits for them, and re-layouts  3.34 us (7%)
  between operations  0.68 us (1%)
    pallas_call x1, Pallas kernels, on_device(): pl.pallas_call(functools.partial(relax_kernel, n_gz, n_gx), out_shape=(ja...  46.3 us
    unnamed x10, local copies, waits for them, and re-layouts  3.34 us

profile of v6, /device:TPU:0, one launch (start us, length us, event | category | flops | bytes accessed | tf_op | source)
XLA Modules:
  0.0 50.5 jit_solution(14403468023274847122)
XLA Ops:
  0.7 0.0 copy-start.1
  0.7 0.0 copy-start.2
  0.7 0.0 copy-start.3
  0.7 0.2 and_select_fusion.pool_ref
  0.9 0.5 copy-done.1
  1.4 0.0 copy-done.2
  1.4 0.0 copy-done.3
  1.4 0.0 copy-start
  1.4 1.2 %copy-done = f32[64,32,128]{2,1,0:T(8,128)S(1)} copy-done((f32[64,32,128]{2,1,0:T(8,128)S(1)}, f32[64,32,128]{2,1,0:T(8,128)}, u32[]{:S(2)}) %copy-start) | copy-done | bytes 1048600
  2.6 46.3 %shard_map.59 = (f32[64,32,128]{2,1,0:T(8,128)S(1)}, f32[32,1024]{1,0:T(8,128)S(1)}) custom-call(f32[64,32,128]{2,1,0:T(8,128)S(1)} %copy-done, s32[32,128]{1,0:T(8,128)S(1)} %bitcast.1, f32[256]{0:T(256)S(1)} %copy-done.2, s32[1,32]{1,0:T(1,128)S(1)} %copy-done.3, f32[512,256]{1,0:T(8,128)S(1)} %and_select_fusion.pool_ref), custom_call_target="tpu_custom_call" | custom-call | tf_op jit(solution)/shard_map/pallas_call | solution.py:423
  48.9 1.0 %copy.8 = f32[64,32,128]{2,1,0:T(8,128)} copy(f32[64,32,128]{2,1,0:T(8,128)S(1)} %get-tuple-element.8) | data formatting | bytes 2097152
  49.9 0.7 %copy.9 = f32[32,1024]{1,0:T(8,128)} copy(f32[32,1024]{1,0:T(8,128)S(1)} %get-tuple-element.9) | data formatting | bytes 262144
  (2 shorter events, 0.0 us)
Async XLA Ops:
  0.7 0.7 %copy-start.1 = (s32[128,32]{0,1:T(8,128)S(1)}, s32[128,32]{0,1:T(8,128)}, u32[]{:S(2)}) copy-start(s32[128,32]{0,1:T(8,128)} %param.5) | copy-start | bytes 49156
  0.7 0.7 %copy-start.2 = (f32[256]{0:T(256)S(1)}, f32[256]{0:T(256)}, u32[]{:S(2)}) copy-start(f32[256]{0:T(256)} %coef_ref.1) | copy-start | bytes 3076
  0.7 0.7 %copy-start.3 = (s32[1,32]{1,0:T(1,128)S(1)}, s32[1,32]{1,0:T(1,128)}, u32[]{:S(2)}) copy-start(s32[1,32]{1,0:T(1,128)} %balance_ref.1) | copy-start | bytes 388
  1.4 1.2 %copy-start = (f32[64,32,128]{2,1,0:T(8,128)S(1)}, f32[64,32,128]{2,1,0:T(8,128)}, u32[]{:S(2)}) copy-start(f32[64,32,128]{2,1,0:T(8,128)} %rhs_ref.1) | copy-start | bytes 3145732

commit v7 on v5

--- a/solution.py
+++ b/solution.py
@@ -9,7 +9,7 @@
 
 SWEEPS = 2
 SOLVES = 2 * SWEEPS
-UNROLL = 8
+UNROLL = 16
 MESH = pl.DeviceIdType.MESH
 
 

time: 50.8 us -> 49 us (0.965)
  Pallas kernels: 46.3 us -> 44.5 us
    pallas_call x1, Pallas kernels: 46.3 us -> 44.5 us  [on_device(): pl.pallas_call(functools.partial(relax_kernel, n_gz, n_gx), out_shape=(ja...]
where the time goes in v7:
time: 49 us; the launch traced here: 48.7 us
  Pallas kernels  44.5 us (91%)
  local copies, waits for them, and re-layouts  3.34 us (7%)
  between operations  0.68 us (1%)
    pallas_call x1, Pallas kernels, on_device(): pl.pallas_call(functools.partial(relax_kernel, n_gz, n_gx), out_shape=(ja...  44.5 us
    unnamed x10, local copies, waits for them, and re-layouts  3.34 us

profile of v7, /device:TPU:0, one launch (start us, length us, event | category | flops | bytes accessed | tf_op | source)
XLA Modules:
  0.0 48.7 jit_solution(14077173571977066561)
XLA Ops:
  0.7 0.0 copy-start.1
  0.7 0.0 copy-start.2
  0.7 0.0 copy-start.3
  0.7 0.2 and_select_fusion.pool_ref
  0.9 0.5 copy-done.1
  1.4 0.0 copy-done.2
  1.4 0.0 copy-done.3
  1.4 0.0 copy-start
  1.4 1.2 %copy-done = f32[64,32,128]{2,1,0:T(8,128)S(1)} copy-done((f32[64,32,128]{2,1,0:T(8,128)S(1)}, f32[64,32,128]{2,1,0:T(8,128)}, u32[]{:S(2)}) %copy-start) | copy-done | bytes 1048600
  2.6 44.5 %shard_map.59 = (f32[64,32,128]{2,1,0:T(8,128)S(1)}, f32[32,1024]{1,0:T(8,128)S(1)}) custom-call(f32[64,32,128]{2,1,0:T(8,128)S(1)} %copy-done, s32[32,128]{1,0:T(8,128)S(1)} %bitcast.1, f32[256]{0:T(256)S(1)} %copy-done.2, s32[1,32]{1,0:T(1,128)S(1)} %copy-done.3, f32[512,256]{1,0:T(8,128)S(1)} %and_select_fusion.pool_ref), custom_call_target="tpu_custom_call" | custom-call | tf_op jit(solution)/shard_map/pallas_call | solution.py:421
  47.1 1.0 %copy.8 = f32[64,32,128]{2,1,0:T(8,128)} copy(f32[64,32,128]{2,1,0:T(8,128)S(1)} %get-tuple-element.8) | data formatting | bytes 2097152
  48.1 0.7 %copy.9 = f32[32,1024]{1,0:T(8,128)} copy(f32[32,1024]{1,0:T(8,128)S(1)} %get-tuple-element.9) | data formatting | bytes 262144
  (2 shorter events, 0.0 us)
Async XLA Ops:
  0.7 0.7 %copy-start.1 = (s32[128,32]{0,1:T(8,128)S(1)}, s32[128,32]{0,1:T(8,128)}, u32[]{:S(2)}) copy-start(s32[128,32]{0,1:T(8,128)} %param.5) | copy-start | bytes 49156
  0.7 0.7 %copy-start.2 = (f32[256]{0:T(256)S(1)}, f32[256]{0:T(256)}, u32[]{:S(2)}) copy-start(f32[256]{0:T(256)} %coef_ref.1) | copy-start | bytes 3076
  0.7 0.7 %copy-start.3 = (s32[1,32]{1,0:T(1,128)S(1)}, s32[1,32]{1,0:T(1,128)}, u32[]{:S(2)}) copy-start(s32[1,32]{1,0:T(1,128)} %balance_ref.1) | copy-start | bytes 388
  1.4 1.2 %copy-start = (f32[64,32,128]{2,1,0:T(8,128)S(1)}, f32[64,32,128]{2,1,0:T(8,128)}, u32[]{:S(2)}) copy-start(f32[64,32,128]{2,1,0:T(8,128)} %rhs_ref.1) | copy-start | bytes 3145732
